TPU v7x, 32 devices: a whole 2x2x4 slice. The times are simulated.
32 devices in a mesh: groups: 2 (over y), tm: 16 (over z, x, core).
Axes of the slice: x: 2, y: 2, z: 4, core: 2. Of those that a mesh axis runs over, the one named last changes fastest.
Arguments:
- observations: float32 [32, 128], P(('groups', 'tm')), parts along dimension 0, may hold values from -6 to 6
- noise_var: float32 [32, 128], P(('groups', 'tm')), parts along dimension 0, may hold values from 0.05 to 2
- gauge_index: int32 [256], P('groups'), parts along dimension 0, may hold values from 0 to 255, as said below
- dynamics: float32 [256, 256], replicated
- process: float32 [256, 256], replicated
Outputs:
- filtered: float32 [32, 256], P(('groups', 'tm')), parts along dimension 0
- filtered_cov: float32 [32, 256, 256], P(('groups', 'tm')), parts along dimension 0
- smoothed: float32 [32, 256], P(('groups', 'tm')), parts along dimension 0
There are 2 independent parts, one for each index of `groups`. A program takes and returns all parts, laid end to end along the dimension named above; an argument that names none is the same for every part. Nothing has to cross between parts.
Inputs may be any that keep to these rules, and one draw needn't show every extreme that they name: `gauge_index`: the 128 numbers are distinct.
All inputs are finite; a program needn't handle non-finite values.
Results may differ from a plain program's by a relative error of at most 0.00015.
Values sent between devices are 32-bit elements; how exact they have to be, the bound alone decides.
A program may use at most 256 MiB of HBM per device.

v0:
```python
import jax
import jax.numpy as jnp
from jax import lax
from jax.sharding import PartitionSpec as P

HIGHEST = lax.Precision.HIGHEST


def carried_in(part, axis, combine, identity, reverse):
    count = lax.axis_size(axis)
    place = lax.axis_index(axis)
    ahead = count - 1 - place if reverse else place
    gathered = jax.tree.map(lambda a: lax.all_gather(a, axis), part)
    state = jax.tree.map(lambda a, e: jnp.zeros_like(a) + jnp.asarray(e, a.dtype), part, identity)

    def one(step, state):
        source = count - 1 - step if reverse else step
        return combine(
            state, jax.tree.map(lambda a: lax.dynamic_index_in_dim(a, source, 0, False), gathered)
        )

    return lax.fori_loop(0, ahead, one, state)


def matmul(left, right):
    return jnp.matmul(left, right, precision=HIGHEST)


def chol_solve(factor, rhs):
    column = rhs.ndim == 1
    block_rhs = rhs[:, None] if column else rhs
    half_solved = lax.linalg.triangular_solve(factor, block_rhs, left_side=True, lower=True)
    full_solved = lax.linalg.triangular_solve(
        factor, half_solved, left_side=True, lower=True, transpose_a=True
    )
    return full_solved[:, 0] if column else full_solved


def selector_matrix(gauge_index, states):
    return (gauge_index[:, None] == jnp.arange(states, dtype=jnp.int32)[None, :]).astype(
        jnp.float32
    )


def filter_step(carried, inputs, selector, dynamics, process):
    state_mean, state_cov = carried
    obs_row, var_row = inputs
    pred_mean = matmul(dynamics, state_mean)
    pred_cov = matmul(matmul(dynamics, state_cov), dynamics.T) + process
    sel_cov = matmul(selector, pred_cov)
    innovation = matmul(sel_cov, selector.T) + jnp.diag(var_row)
    factor = jnp.linalg.cholesky(innovation)
    solved = chol_solve(factor, sel_cov)
    residual = obs_row - matmul(selector, pred_mean)
    new_mean = pred_mean + matmul(solved.T, residual)
    new_cov = pred_cov - matmul(sel_cov.T, solved)
    return ((new_mean, new_cov), (new_mean, new_cov))


def smoother_gain(state_cov, dynamics, process):
    propagated = matmul(dynamics, state_cov)
    predicted = matmul(propagated, dynamics.T) + process
    factor = jnp.linalg.cholesky(predicted)
    return chol_solve(factor, propagated).T


def combine_filter(first_part, second_part):
    trans_first, offset_first, cov_first, info_first, prec_first, empty_first = first_part
    trans_second, offset_second, cov_second, info_second, prec_second, empty_second = second_part
    identity = jnp.eye(cov_first.shape[-1], dtype=jnp.float32)
    root_first = jnp.linalg.cholesky(cov_first + empty_first * identity)
    inner_matrix = identity + matmul(matmul(root_first.T, prec_second), root_first)
    inner_root = jnp.linalg.cholesky(inner_matrix)
    whitened = lax.linalg.triangular_solve(inner_root, root_first.T, left_side=True, lower=True)
    middle = matmul(whitened.T, whitened)
    guided_trans = trans_first - matmul(middle, matmul(prec_second, trans_first))
    transition = matmul(trans_second, guided_trans)
    guided_offset = (
        offset_first
        - matmul(middle, matmul(prec_second, offset_first))
        + matmul(middle, info_second)
    )
    offset_new = matmul(trans_second, guided_offset) + offset_second
    cov_new = matmul(matmul(trans_second, middle), trans_second.T) + cov_second
    info_residue = info_second - matmul(prec_second, offset_first)
    info_new = (
        matmul(trans_first.T, info_residue - matmul(prec_second, matmul(middle, info_residue)))
        + info_first
    )
    prec_middle = prec_second - matmul(matmul(prec_second, middle), prec_second)
    prec_new = matmul(matmul(trans_first.T, prec_middle), trans_first) + prec_first
    computed = (transition, offset_new, cov_new, info_new, prec_new, empty_first * empty_second)

    def select(first_leaf, second_leaf, computed_leaf):
        keep_first = jnp.where(empty_second > 0.5, first_leaf, computed_leaf)
        return jnp.where(empty_first > 0.5, second_leaf, keep_first)

    return jax.tree.map(select, first_part, second_part, computed)


def combine_smooth(first_part, second_part):
    gain_first, offset_first = first_part
    gain_second, offset_second = second_part
    return (matmul(gain_second, gain_first), matmul(gain_second, offset_first) + offset_second)


def shards(observations, noise_var, gauge_index, dynamics, process):
    states = dynamics.shape[0]
    step_count = observations.shape[0]
    identity = jnp.eye(states, dtype=jnp.float32)
    selector = selector_matrix(gauge_index, states)
    sel_process = matmul(selector, process)
    sel_dynamics = matmul(selector, dynamics)
    sel_square = matmul(sel_process, selector.T)

    def element(obs_row, var_row):
        innovation = sel_square + jnp.diag(var_row)
        factor = jnp.linalg.cholesky(innovation)
        kalman_gain = chol_solve(factor, sel_process).T
        transition = dynamics - matmul(kalman_gain, sel_dynamics)
        offset_vec = matmul(kalman_gain, obs_row)
        covariance = process - matmul(kalman_gain, sel_process)
        information = matmul(sel_dynamics.T, chol_solve(factor, obs_row))
        precision_mat = matmul(sel_dynamics.T, chol_solve(factor, sel_dynamics))
        return (
            transition,
            offset_vec,
            covariance,
            information,
            precision_mat,
            jnp.zeros((), jnp.float32),
        )

    elements = jax.vmap(element)(observations, noise_var)
    first_element = jax.tree.map(lambda array_leaf: array_leaf[0], elements)
    rest_elements = jax.tree.map(lambda array_leaf: array_leaf[1:], elements)

    def accumulate(carried, incoming):
        merged = combine_filter(carried, incoming)
        return (merged, merged)

    summary, later_prefixes = lax.scan(accumulate, first_element, rest_elements)
    zero_vector = jnp.zeros((states,), jnp.float32)
    zero_matrix = jnp.zeros((states, states), jnp.float32)
    neutral = (
        identity,
        zero_vector,
        zero_matrix,
        zero_vector,
        zero_matrix,
        jnp.ones((), jnp.float32),
    )
    prefix = carried_in(summary, "tm", combine_filter, neutral, False)

    def advance(carried, inputs):
        return filter_step(carried, inputs, selector, dynamics, process)

    final_state, outputs = lax.scan(advance, (prefix[1], prefix[2]), (observations, noise_var))
    filtered_means, filtered_covs = outputs
    gains = jax.vmap(lambda one_cov: smoother_gain(one_cov, dynamics, process))(filtered_covs)
    position = jnp.arange(step_count, dtype=jnp.int32)
    at_end = jnp.logical_and(
        lax.axis_index("tm") == lax.axis_size("tm") - 1, position == step_count - 1
    )
    gains = gains * (1.0 - at_end.astype(jnp.float32))[:, None, None]
    moved_means = jnp.einsum("ij,tj->ti", dynamics, filtered_means, precision=HIGHEST)
    offsets = filtered_means - jnp.einsum("tij,tj->ti", gains, moved_means, precision=HIGHEST)

    def compose(carried, inputs):
        block_gain, block_offset = carried
        step_gain, step_offset = inputs
        return (
            (matmul(step_gain, block_gain), matmul(step_gain, block_offset) + step_offset),
            None,
        )

    block_map, nothing = lax.scan(
        compose, (gains[-1], offsets[-1]), (gains[:-1], offsets[:-1]), reverse=True
    )
    suffix = carried_in(block_map, "tm", combine_smooth, (identity, zero_vector), True)

    def retreat(carried, inputs):
        step_gain, step_offset = inputs
        smoothed_now = matmul(step_gain, carried) + step_offset
        return (smoothed_now, smoothed_now)

    final_value, smoothed = lax.scan(retreat, suffix[1], (gains, offsets), reverse=True)
    return (filtered_means, filtered_covs, smoothed)


def solution(mesh):
    return jax.shard_map(
        shards,
        mesh=mesh,
        in_specs=(P(("groups", "tm"), None), P(("groups", "tm"), None), P("groups"), P(), P()),
        out_specs=(
            P(("groups", "tm"), None),
            P(("groups", "tm"), None, None),
            P(("groups", "tm"), None),
        ),
        check_vma=False,
    )
```

profile of v0, /device:TPU:0, one launch (start us, length us, event | category | flops | bytes accessed | tf_op | source)
XLA Modules:
  0.0 2029.4 jit_solution(3023154063241289294)
XLA Ops:
  7.2 1.3 fusion.81
  8.5 1.0 fusion.61
  9.6 11.7 custom-call.55
  21.4 0.6 compare_reduce_fusion.7
  22.0 0.7 fusion.82
  22.7 9.8 custom-call.68
  33.1 1.2 fusion.80
  34.3 2.1 convolution_subtract_fusion.5
  37.0 1.1 fusion.121
  38.2 1.1 convolution_subtract_fusion.4
  40.1 0.8 dynamic-update-slice.26
  40.8 35.5 %all-reduce.2 = f32[16]{0:T(128)S(1)} all-reduce(f32[16]{0:T(128)S(1)} %dynamic-update-slice.26), channel_id=1, replica_groups=mesh['groups'=2,'tm'=16] {'tm'}, use_global_device_ids=true, to_apply=%add.2 | all-reduce | flops 16 | bytes 128
  76.6 17.2 all-gather.6
  94.3 19.3 all-gather.7
  113.6 27.7 %all-gather.18.cloned.1.call-done = f32[4096,256]{1,0:T(8,128)} async-done(((f32[256,256]{1,0:T(8,128)}), f32[4096,256]{1,0:T(8,128)}) %all-gather.18.cloned.1.call-update) | async-done | bytes 4194320 | tf_op jit(solution)/shard_map/all_gather | solution.py:13
  141.3 51.3 %all-gather.20.cloned.1.call-done = f32[4096,256]{1,0:T(8,128)} async-done(((f32[256,256]{1,0:T(8,128)}), f32[4096,256]{1,0:T(8,128)}) %all-gather.20.cloned.1.call-update) | async-done | bytes 4194320 | tf_op jit(solution)/shard_map/all_gather | solution.py:13
  192.8 0.7 copy-done
  195.4 11.7 cholesky.157
  207.1 0.6 compare_reduce_fusion.6
  207.8 0.7 fusion.83
  208.4 9.8 custom-call.57
  220.5 11.9 custom-call.58
  232.4 9.8 custom-call.59
  242.7 11.7 custom-call.60
  254.5 0.6 compare_reduce_fusion.4
  256.5 4.0 while.24
  257.1 1.4 bitcast_dynamic-update-slice_fusion.5
  259.1 1.4 bitcast_dynamic-update-slice_fusion.5
  260.5 19.7 custom-call.61
  282.2 0.8 copy.43
  284.3 1685.3 %all-gather.8 = f32[16,1,256]{2,1,0:T(1,128)S(1)} all-gather(f32[1,1,256]{2,1,0:T(1,128)S(1)} %bitcast.428), channel_id=7, replica_groups=mesh['groups'=2,'tm'=16] {'tm'}, dimensions={0}, use_global_device_ids=true | all-gather | bytes 17408 | tf_op jit(solution)/shard_map/all_gather | solution.py:13
  1969.6 32.5 %all-gather.14.cloned.1.call-done = f32[16,256,256]{2,1,0:T(8,128)} async-done(((f32[1,256,256]{2,1,0:T(8,128)}), f32[16,256,256]{2,1,0:T(8,128)}) %all-gather.14.cloned.1.call-update) | async-done | bytes 4194320 | tf_op jit(solution)/shard_map/all_gather | solution.py:13
  2002.2 19.9 while.23
  2002.2 1.2 fusion.270
  2003.5 1.2 fusion.270
  2004.8 1.2 fusion.270
  2006.1 1.2 fusion.270
  2007.5 1.2 fusion.270
  2008.8 1.2 fusion.270
  2010.1 1.2 fusion.270
  2011.4 1.2 fusion.270
  2012.8 1.2 fusion.270
  2014.1 1.2 fusion.270
  2015.4 1.2 fusion.270
  2016.7 1.2 fusion.270
  2018.1 1.2 fusion.270
  2019.4 1.2 fusion.270
  2020.7 1.2 fusion.270
  (119 shorter events, 14.0 us)
Async XLA Ops:
  7.2 32.3 %copy-start.7 = (u32[32]{0:T(128)S(1)}, u32[32]{0:T(128)}, u32[]{:S(2)}) copy-start(u32[32]{0:T(128)} %constant.386) | copy-start | bytes 388
  7.2 31.1 %copy-start.1 = (f32[256,256]{1,0:T(8,128)S(1)}, f32[256,256]{1,0:T(8,128)}, u32[]{:S(2)}) copy-start(f32[256,256]{1,0:T(8,128)} %param.18) | copy-start | bytes 786436
  7.2 69.3 %copy-start.6 = (f32[1,128]{1,0:T(1,128)S(1)}, f32[1,128]{1,0:T(1,128)}, u32[]{:S(2)}) copy-start(f32[1,128]{1,0:T(1,128)} %param.14) | copy-start | bytes 1540
  7.2 106.4 %all-gather.16.cloned.1.call-start = ((), (), s32[]{:S(2)}) async-start(), calls=%async_computation.1 | async-start | bytes 4456448 | tf_op jit(solution)/shard_map/all_gather | solution.py:13
  36.4 104.9 %all-gather.18.cloned.1.call-start = ((), (), s32[]{:S(2)}) async-start(), calls=%async_computation.2 | async-start | bytes 4456448 | tf_op jit(solution)/shard_map/all_gather | solution.py:13
  38.2 154.4 %all-gather.20.cloned.1.call-start = ((), (), s32[]{:S(2)}) async-start(), calls=%async_computation.3 | async-start | bytes 4456448 | tf_op jit(solution)/shard_map/all_gather | solution.py:13
  39.4 1962.8 %all-gather.14.cloned.1.call-start = ((), (), s32[]{:S(2)}) async-start(), calls=%async_computation | async-start | bytes 4456448 | tf_op jit(solution)/shard_map/all_gather | solution.py:13
  192.6 1.0 copy-start
  192.6 2.0 copy-start.3
  192.6 2.6 copy-start.5
  219.2 62.9 %copy-start.2 = (f32[256,256]{1,0:T(8,128)}, f32[256,256]{1,0:T(8,128)S(1)}, u32[]{:S(2)}) copy-start(f32[256,256]{1,0:T(8,128)S(1)} %convolution_subtract_fusion.3) | copy-start | bytes 786436
  283.8 1739.1 %copy-start.4 = (f32[256]{0:T(256)}, f32[256]{0:T(256)S(1)}, u32[]{:S(2)}) copy-start(f32[256]{0:T(256)S(1)} %add.177) | copy-start | bytes 3076
Sparse Core Ops, SparseCore 0:
  36.5 53.4 all-gather.15
  92.1 49.1 all-gather.17
  143.5 49.0 all-gather.19
  283.1 1718.9 all-gather.13
where the time goes:
time: 2040 us; the launch traced here: 2030 us
  blocking collectives  1760 us (86%)
  waiting for transfers between devices  112 us (5%)
  other arithmetic  100 us (5%)
  matrix products  35.4 us (2%)
    all_gather x3, blocking collectives, carried_in(): gathered = jax.tree.map(lambda a: lax.all_gather(a, axis), part)  1720 us
    all_gather x4, waiting for transfers between devices, carried_in(): gathered = jax.tree.map(lambda a: lax.all_gather(a, axis), part)  111 us
  transfers between devices with their start and end apart: 4, of which 3 were waited for; matrix products, arithmetic and copies ran while one was open for 0% of the time, Pallas kernels for 0%

commit v1 on v0

v1 whole, which is shorter than its diff:
```python
import functools

import jax
import jax.numpy as jnp
from jax import lax
from jax.experimental import pallas as pl
from jax.experimental.pallas import tpu as pltpu
from jax.sharding import PartitionSpec as P

F32 = jnp.float32
BF16 = jnp.bfloat16
HIGHEST = lax.Precision.HIGHEST
RESIDUAL_LIMIT = 1e-4


def split(a):
    high = a.astype(BF16)
    return high, (a - high.astype(F32)).astype(BF16)


def dot(a, b):
    return jnp.dot(a, b, preferred_element_type=F32)


def dot3(a, b):
    (ah, al), (bh, bl) = a, b
    return dot(
        jnp.concatenate([ah, ah, al], axis=1), jnp.concatenate([bh, bl, bh], axis=0)
    )


def dot_t(a, b):
    return lax.dot_general(a, b, (((1,), (1,)), ((), ())), preferred_element_type=F32)


def full(a, b):
    return jnp.dot(a, b, precision=HIGHEST, preferred_element_type=F32)


def iotas(shape):
    return (
        lax.broadcasted_iota(jnp.int32, shape, 0),
        lax.broadcasted_iota(jnp.int32, shape, 1),
    )


def permutation(index_row, states, gauges):
    rows, cols = iotas((states, gauges))
    gauged = (rows == index_row).astype(F32)
    free = 1.0 - jnp.sum(gauged, axis=1, keepdims=True)
    r, c = iotas((states, states))
    below = (c < r).astype(F32)
    rank = dot(below, jnp.broadcast_to(free, (states, gauges)))
    others = jnp.where(rank == cols.astype(F32), free, 0.0)
    return jnp.concatenate([gauged, others], axis=1)


def kernel(
    steps,
    gathered_ref,
    index_ref,
    dynamics_ref,
    process_ref,
    filtered_ref,
    cov_ref,
    smoothed_ref,
    f_ref,
    fh_ref,
    ft_ref,
    q_ref,
    perm_ref,
    pred_ref,
    gain_ref,
    resid_ref,
    kept_ref,
    kept_rows_ref,
    work_ref,
):
    states = dynamics_ref.shape[0]
    gauges = index_ref.shape[1]
    me = lax.axis_index("tm")
    rg, cg = iotas((gauges, gauges))
    eye = (rg == cg).astype(F32)

    perm_t = permutation(index_ref[...], states, gauges)
    perm = perm_t.T
    perm_ref[...] = perm
    f = full(full(perm, dynamics_ref[...]), perm_t)
    f_ref[...] = f
    ft = f.T
    ft_h, ft_l = split(ft)
    ft_ref[0], ft_ref[1] = ft_h, ft_l
    f_h, f_l = split(f)
    fh_ref[0], fh_ref[1] = f_h, f_l
    q_ref[...] = full(full(perm, process_ref[...]), perm_t)

    def gauss_jordan(s):
        work_ref[...] = s

        def pivot(k, nothing):
            m = work_ref[...]
            row = jnp.sum(jnp.where(rg == k, m, 0.0), axis=0, keepdims=True)
            col = jnp.sum(jnp.where(cg == k, m, 0.0), axis=1, keepdims=True)
            inv = 1.0 / jnp.sum(jnp.where(cg[:1] == k, row, 0.0), axis=1, keepdims=True)
            scaled = row * inv
            new = m - col * scaled
            new = jnp.where(cg == k, -col * inv, new)
            new_row = jnp.where(cg[:1] == k, inv, scaled)
            work_ref[...] = jnp.where(rg == k, new_row, new)
            return nothing

        lax.fori_loop(0, gauges, pivot, 0)
        return work_ref[...]

    def run(robust):
        mm = full if robust else (lambda a, b: dot3(split(a), split(b)))
        pred_ref[...] = q_ref[...]

        def forward(t, carried):
            x, worst = carried
            obs = gathered_ref[t][:, :gauges]
            r_row = gathered_ref[t][:, gauges:]
            r_col = jnp.sum(eye * r_row, axis=1, keepdims=True)
            s = pred_ref[:gauges, :gauges] + eye * r_row
            diag = eye * s
            d_row = lax.rsqrt(jnp.sum(diag, axis=0, keepdims=True))
            d_col = lax.rsqrt(jnp.sum(diag, axis=1, keepdims=True))
            scaled = s * d_col * d_row
            b = d_col * pred_ref[:gauges, gauges:]
            if robust:
                inverse = gauss_jordan(scaled)
                both = jnp.concatenate([inverse, full(inverse, b)], axis=1)
            else:
                e = eye - scaled
                e1 = e.astype(BF16)
                e2 = dot(e1, e1)
                e2b = e2.astype(BF16)
                e34 = dot(e2b, jnp.concatenate([e1, e2b], axis=1))
                y3 = eye + e + e2 + e34[:, :gauges]
                x7 = y3 + dot(e34[:, gauges:].astype(BF16), y3.astype(BF16))
                xs = split(x7)
                prod = dot3(xs, split(jnp.concatenate([e, b], axis=1)))
                residual = eye - x7 + prod[:, :gauges]
                half = prod[:, gauges:]
                both = jnp.concatenate([x7, half], axis=1) + dot(
                    residual.astype(BF16),
                    jnp.concatenate([xs[0], half.astype(BF16)], axis=1),
                )
                worst = jnp.maximum(
                    worst, jnp.sum(residual * residual, axis=0, keepdims=True)
                )
            w = both[:, :gauges] * d_col * d_row
            vt = both[:, gauges:] * d_col
            gain = jnp.concatenate([w, vt], axis=1)
            gain_ref[t] = gain
            y = obs - x[:, :gauges]
            resid_ref[t] = y
            gy = mm(jnp.broadcast_to(y, (8, gauges)), gain)[:1]
            mean = jnp.concatenate(
                [obs - r_row * gy[:, :gauges], x[:, gauges:] + gy[:, gauges:]], axis=1
            )
            p_ou = vt * r_col
            p_oo = eye * r_row - w * r_col * r_row
            p_uu = pred_ref[gauges:, gauges:] - mm(pred_ref[gauges:, :gauges], vt)
            cov = jnp.concatenate(
                [
                    jnp.concatenate([p_oo, p_ou], axis=1),
                    jnp.concatenate([p_ou.T, p_uu], axis=1),
                ],
                axis=0,
            )
            slot = jnp.where(t == me, 0, 1)
            kept_ref[slot] = cov
            kept_rows_ref[slot] = jnp.broadcast_to(mean, (8, states))
            stacked = jnp.concatenate([cov, jnp.broadcast_to(mean, (16, states))], axis=0)
            if robust:
                moved = full(stacked, f_ref[...].T)
                pred_ref[...] = full(f_ref[...], moved[:states]) + q_ref[...]
            else:
                moved = dot3(split(stacked), (ft_ref[0], ft_ref[1]))
                pred_ref[...] = (
                    dot3((fh_ref[0], fh_ref[1]), split(moved[:states])) + q_ref[...]
                )
            return moved[states : states + 1], worst

        zero = jnp.zeros((1, states), F32)
        nothing, worst = lax.fori_loop(
            0, steps, forward, (zero, jnp.zeros((1, gauges), F32))
        )

        def backward(i, lam):
            t = steps - 1 - i
            slot = jnp.where(t == me, 2, 3)
            kept_rows_ref[slot] = jnp.broadcast_to(lam, (8, states))
            r_row = gathered_ref[t][:, gauges:]
            y = resid_ref[t]
            z = jnp.concatenate([r_row * lam[:, :gauges] - y, -lam[:, gauges:]], axis=1)
            z = jnp.broadcast_to(z, (8, states))
            if robust:
                new = full(z, gain_ref[t].T)[:1]
            else:
                zh, zl = split(z)
                gh, gl = split(gain_ref[t])
                new = (dot_t(zh, gh) + (dot_t(zh, gl) + dot_t(zl, gh)))[:1]
            joined = jnp.broadcast_to(
                jnp.concatenate([new, lam[:, gauges:]], axis=1), (8, states)
            )
            if robust:
                return full(joined, f_ref[...])[:1]
            return dot3(split(joined), (fh_ref[0], fh_ref[1]))[:1]

        lax.fori_loop(0, steps, backward, zero)
        return jnp.sum(worst)

    worst = run(False)

    @pl.when(jnp.logical_not(worst < RESIDUAL_LIMIT))
    def _():
        run(True)

    perm = perm_ref[...]
    cov = kept_ref[0]
    cov_ref[0] = full(full(perm.T, cov), perm)
    mean, lam = kept_rows_ref[0], kept_rows_ref[2]
    smooth = mean - full(lam, cov)
    filtered_ref[...] = full(mean, perm)[:1]
    smoothed_ref[...] = full(smooth, perm)[:1]


def shards(observations, noise_var, gauge_index, dynamics, process):
    states = dynamics.shape[0]
    gauges = gauge_index.shape[0]
    packed = jnp.concatenate([observations, noise_var], axis=1)
    gathered = lax.all_gather(packed, "tm")
    steps = gathered.shape[0]
    vmem = pl.BlockSpec(memory_space=pltpu.VMEM)
    return pl.pallas_call(
        functools.partial(kernel, steps),
        out_shape=(
            jax.ShapeDtypeStruct((1, states), F32),
            jax.ShapeDtypeStruct((1, states, states), F32),
            jax.ShapeDtypeStruct((1, states), F32),
        ),
        in_specs=[vmem] * 4,
        out_specs=(vmem,) * 3,
        scratch_shapes=[
            pltpu.VMEM((states, states), F32),
            pltpu.VMEM((2, states, states), BF16),
            pltpu.VMEM((2, states, states), BF16),
            pltpu.VMEM((states, states), F32),
            pltpu.VMEM((states, states), F32),
            pltpu.VMEM((states, states), F32),
            pltpu.VMEM((steps, gauges, states), F32),
            pltpu.VMEM((steps, 1, gauges), F32),
            pltpu.VMEM((2, states, states), F32),
            pltpu.VMEM((4, 8, states), F32),
            pltpu.VMEM((gauges, gauges), F32),
        ],
        compiler_params=pltpu.CompilerParams(vmem_limit_bytes=48 * 1024 * 1024),
    )(gathered, gauge_index.reshape(1, gauges), dynamics, process)


def solution(mesh):
    return jax.shard_map(
        shards,
        mesh=mesh,
        in_specs=(P(("groups", "tm"), None), P(("groups", "tm"), None), P("groups"), P(), P()),
        out_specs=(
            P(("groups", "tm"), None),
            P(("groups", "tm"), None, None),
            P(("groups", "tm"), None),
        ),
        check_vma=False,
    )
```

time: 2040 us -> 62.6 us (0.03)
  blocking collectives: 1760 us -> 23.2 us
  waiting for transfers between devices: 112 us -> 0 us
  other arithmetic: 100 us -> 0.01 us
  Pallas kernels: 0 us -> 36 us
  matrix products: 35.4 us -> 0 us
    all_gather x3 -> x1, blocking collectives: 1720 us -> 23.2 us  [shards(): gathered = lax.all_gather(packed, 'tm')]
    all_gather x4 -> x0, waiting for transfers between devices: 111 us -> none  [carried_in(): gathered = jax.tree.map(lambda a: lax.all_gather(a, axis), part)]
    another operation x19 -> x0, other arithmetic: 99.6 us -> none  [the longest x7 40.6 us: chol_solve(): lax.linalg.triangular_solve(factor, half_solved, left_side=True, lower=Tr...]
    pallas_call x0 -> x1, Pallas kernels: none -> 36 us  [shards(): pl.pallas_call(functools.partial(kernel, steps), out_shape=(jax.ShapeDtyp...]
    unnamed x1 -> x0, blocking collectives: 35.5 us -> none
    dot_general x36 -> x0, matrix products: 31 us -> none  [the longest x34 30.4 us: matmul(): return jnp.matmul(left, right, precision=HIGHEST)]
  transfers between devices with their start and end apart: 4 -> 0, of which waited for: 3 -> 0; matrix products, arithmetic and copies ran while one was open for 0% -> 0% of each run, Pallas kernels for 0% -> 0%
where the time goes in v1:
time: 62.6 us; the launch traced here: 62.4 us
  Pallas kernels  36 us (58%)
  blocking collectives  23.2 us (37%)
  local copies, waits for them, and re-layouts  2.56 us (4%)
  between operations  0.65 us (1%)
    pallas_call x1, Pallas kernels, shards(): pl.pallas_call(functools.partial(kernel, steps), out_shape=(jax.ShapeDtyp...  36 us
    all_gather x1, blocking collectives, shards(): gathered = lax.all_gather(packed, 'tm')  23.2 us
    unnamed x10, local copies, waits for them, and re-layouts  2.56 us

profile of v1, /device:TPU:0, one launch (start us, length us, event | category | flops | bytes accessed | tf_op | source)
XLA Modules:
  0.0 62.4 jit_solution(9613656167161161671)
XLA Ops:
  0.6 0.0 copy-start.3
  0.6 0.0 copy-start.4
  0.6 0.6 %copy-done.3 = f32[1,128]{1,0:T(1,128)S(1)} copy-done((f32[1,128]{1,0:T(1,128)S(1)}, f32[1,128]{1,0:T(1,128)}, u32[]{:S(2)}) %copy-start.3) | copy-done | bytes 536
  1.3 0.0 copy-done.4
  1.3 0.0 copy-start.2
  1.3 23.2 %all-gather.1.gathered_ref = f32[16,1,256]{2,1,0:T(1,128)S(1)} all-gather(f32[1,1,256]{2,1,0:T(1,128)S(1)} %maximum_bitcast_fusion), channel_id=2, replica_groups=mesh['groups'=2,'tm'=16] {'tm'}, dimensions={0}, use_global_device_ids=true | all-gather | bytes 17408 | tf_op jit(solution)/shard_map/all_gather | solution.py:234
  24.5 0.0 copy-done.2
  24.5 0.0 copy-start
  24.5 0.9 %copy-done = f32[256,256]{1,0:T(8,128)S(1)} copy-done((f32[256,256]{1,0:T(8,128)S(1)}, f32[256,256]{1,0:T(8,128)}, u32[]{:S(2)}) %copy-start) | copy-done | bytes 262168
  25.5 0.0 copy-start.1
  25.5 0.9 %copy-done.1 = f32[256,256]{1,0:T(8,128)S(1)} copy-done((f32[256,256]{1,0:T(8,128)S(1)}, f32[256,256]{1,0:T(8,128)}, u32[]{:S(2)}) %copy-start.1) | copy-done | bytes 262168
  26.4 36.0 %shard_map.76 = (f32[1,256]{1,0:T(1,128)}, f32[1,256,256]{2,1,0:T(8,128)}, f32[1,256]{1,0:T(1,128)}) custom-call(f32[16,1,256]{2,1,0:T(1,128)S(1)} %all-gather.1.gathered_ref, s32[1,128]{1,0:T(1,128)S(1)} %bitcast.3, f32[256,256]{1,0:T(8,128)S(1)} %copy-done, f32[256,256]{1,0:T(8,128)S(1)} %copy-done.1), custom_call_target="tpu_custom_call" | custom-call | tf_op jit(solution)/shard_map/pallas_call | solution.py:237
  (1 shorter events, 0.0 us)
Async XLA Ops:
  0.6 0.7 %copy-start.3 = (f32[1,128]{1,0:T(1,128)S(1)}, f32[1,128]{1,0:T(1,128)}, u32[]{:S(2)}) copy-start(f32[1,128]{1,0:T(1,128)} %param.6) | copy-start | bytes 1540
  0.6 0.7 %copy-start.4 = (f32[1,128]{1,0:T(1,128)S(1)}, f32[1,128]{1,0:T(1,128)}, u32[]{:S(2)}) copy-start(f32[1,128]{1,0:T(1,128)} %param.5) | copy-start | bytes 1540
  1.3 23.2 %copy-start.2 = (s32[128]{0:T(128)S(1)}, s32[128]{0:T(128)}, u32[]{:S(2)}) copy-start(s32[128]{0:T(128)} %param.7) | copy-start | bytes 1540
  24.5 1.0 %copy-start = (f32[256,256]{1,0:T(8,128)S(1)}, f32[256,256]{1,0:T(8,128)}, u32[]{:S(2)}) copy-start(f32[256,256]{1,0:T(8,128)} %dynamics_ref.1) | copy-start | bytes 786436
  25.5 0.9 %copy-start.1 = (f32[256,256]{1,0:T(8,128)S(1)}, f32[256,256]{1,0:T(8,128)}, u32[]{:S(2)}) copy-start(f32[256,256]{1,0:T(8,128)} %process_ref.1) | copy-start | bytes 786436

commit v2 on v1

v2 whole, which is shorter than its diff:
```python
import functools

import jax
import jax.numpy as jnp
import numpy as np
from jax import lax
from jax.experimental import pallas as pl
from jax.experimental.pallas import tpu as pltpu
from jax.sharding import PartitionSpec as P

F32 = jnp.float32
BF16 = jnp.bfloat16
HIGHEST = lax.Precision.HIGHEST
MESH = pl.DeviceIdType.MESH
RADIUS = 0.3
HALF_DEGREE = 4
RESIDUAL_LIMIT = 1e-6


def split(a):
    high = a.astype(BF16)
    return high, (a - high.astype(F32)).astype(BF16)


def dot(a, b):
    return jnp.dot(a, b, preferred_element_type=F32)


def dot3(a, b):
    (ah, al), (bh, bl) = a, b
    return dot(
        jnp.concatenate([ah, ah, al], axis=1), jnp.concatenate([bh, bl, bh], axis=0)
    )


def dot_t(a, b):
    return lax.dot_general(a, b, (((1,), (1,)), ((), ())), preferred_element_type=F32)


def full(a, b):
    return jnp.dot(a, b, precision=HIGHEST, preferred_element_type=F32)


def iotas(shape):
    return (
        lax.broadcasted_iota(jnp.int32, shape, 0),
        lax.broadcasted_iota(jnp.int32, shape, 1),
    )


def permutation(index_row, states, gauges):
    rows, cols = iotas((states, gauges))
    gauged = (rows == index_row).astype(F32)
    free = 1.0 - jnp.sum(gauged, axis=1, keepdims=True)
    r, c = iotas((states, states))
    below = (c < r).astype(F32)
    rank = dot(below, jnp.broadcast_to(free, (states, gauges)))
    others = jnp.where(rank == cols.astype(F32), free, 0.0)
    return jnp.concatenate([gauged, others], axis=1)


def dot3_t(a, b):
    (ah, al), (bh, bl) = a, b
    return dot_t(jnp.concatenate([ah, ah, al], axis=1), jnp.concatenate([bh, bl, bh], axis=1))


def move(a, b):
    if a.dtype == BF16:
        high, low = split(b)
        return dot(a, high) + dot(a, low)
    high, low = split(a)
    return dot(high, b) + dot(low, b)


def factors():
    degree = 2 * HALF_DEGREE
    z = 1.0 / RADIUS
    u = [np.poly1d([1.0]), np.poly1d([2.0, 0.0])]
    for _ in range(degree):
        u.append(np.poly1d([2.0, 0.0]) * u[-1] - u[-2])
    rest = sum((k(z) * k for k in u), np.poly1d([0.0])) / sum(k(z) ** 2 for k in u)
    scaled = np.poly1d([c * z ** (len(rest.coeffs) - 1 - i) for i, c in enumerate(rest.coeffs)])
    quotient, _ = np.polydiv((np.poly1d([1.0]) - scaled).coeffs, np.array([-1.0, 1.0]))
    roots = sorted(np.roots(quotient), key=lambda r: (abs(r.imag) < 1e-9, r.real, r.imag))
    pick = [r for i, r in enumerate(roots) if (i // 2) % 2 == 0]
    other = [r for i, r in enumerate(roots) if (i // 2) % 2 == 1]
    first = np.real(np.poly(pick))
    first = first / first[-1]
    second = np.real(np.poly(other))
    second = second / second[-1] * quotient[-1]
    return [float(c) for c in first[::-1]], [float(c) for c in second[::-1]]


def gather_kernel(count, obs_ref, var_ref, out_ref, row_ref, send_sem, recv_sem):
    me = lax.axis_index("tm")
    group = lax.axis_index("groups")
    gauges = obs_ref.shape[1]
    barrier = pltpu.get_barrier_semaphore()

    def greet(d, nothing):
        peer = lax.rem(me + d, count)
        pl.semaphore_signal(barrier, inc=1, device_id=(group, peer), device_id_type=MESH)
        return nothing

    lax.fori_loop(1, count, greet, 0)
    row_ref[0, :, :gauges] = obs_ref[...]
    row_ref[0, :, gauges:] = var_ref[...]
    out_ref[me] = row_ref[0]
    pl.semaphore_wait(barrier, count - 1)

    def copy(d):
        peer = lax.rem(me + d, count)
        return pltpu.make_async_remote_copy(
            src_ref=row_ref.at[0],
            dst_ref=out_ref.at[me],
            send_sem=send_sem.at[d],
            recv_sem=recv_sem.at[d],
            device_id=(group, peer),
            device_id_type=MESH,
        )

    def start(d, nothing):
        copy(d).start()
        return nothing

    def finish(d, nothing):
        copy(d).wait()
        return nothing

    lax.fori_loop(1, count, start, 0)
    lax.fori_loop(1, count, finish, 0)


def kernel(
    steps,
    gathered_ref,
    index_ref,
    dynamics_ref,
    process_ref,
    filtered_ref,
    cov_ref,
    smoothed_ref,
    f_ref,
    ft_ref,
    q_ref,
    perm_ref,
    perm_t_ref,
    pred_ref,
    gain_ref,
    poly_ref,
    rows_ref,
    kept_ref,
    kept_gain_ref,
    kept_rows_ref,
    work_ref,
):
    states = dynamics_ref.shape[0]
    gauges = index_ref.shape[1]
    me = lax.axis_index("tm")
    rg, cg = iotas((gauges, gauges))
    eye = (rg == cg).astype(F32)
    first, second = factors()

    perm_t = permutation(index_ref[...], states, gauges)
    perm = perm_t.T.astype(BF16)
    perm_t = perm_t.astype(BF16)
    perm_ref[...] = perm
    perm_t_ref[...] = perm_t
    f = move(move(perm, dynamics_ref[...]), perm_t)
    f_ref[0], f_ref[1] = split(f)
    ft_ref[0], ft_ref[1] = split(f.T)
    q_ref[...] = move(move(perm, process_ref[...]), perm_t)

    def gauss_jordan(s):
        work_ref[...] = s

        def pivot(k, nothing):
            m = work_ref[...]
            row = jnp.sum(jnp.where(rg == k, m, 0.0), axis=0, keepdims=True)
            col = jnp.sum(jnp.where(cg == k, m, 0.0), axis=1, keepdims=True)
            inv = 1.0 / jnp.sum(jnp.where(cg[:1] == k, row, 0.0), axis=1, keepdims=True)
            scaled = row * inv
            new = m - col * scaled
            new = jnp.where(cg == k, -col * inv, new)
            new_row = jnp.where(cg[:1] == k, inv, scaled)
            work_ref[...] = jnp.where(rg == k, new_row, new)
            return nothing

        lax.fori_loop(0, gauges, pivot, 0)
        return work_ref[...]

    def step_rows(t):
        row = gathered_ref[t]
        return row[:, :gauges], row[:, gauges:]

    def mean_step(t, x, y):
        g = split(gain_ref[t])
        moved = dot3(split(jnp.broadcast_to(x, (16, states))), (ft_ref[0], ft_ref[1]))
        gy = dot3(split(jnp.broadcast_to(y, (16, gauges))), g)
        rows_ref[t] = gy[:1, :gauges]
        return moved[:1] + gy[:1, gauges:]

    def run(robust):
        pred_ref[...] = q_ref[...]
        gain_ref[0] = jnp.zeros_like(gain_ref[0])

        def forward(t, carried):
            x, y = carried
            x = mean_step(t, x, y)
            obs, r_row = step_rows(t)
            y = obs - x[:, :gauges]
            a = pred_ref[...]
            slot = jnp.where(t == me, 0, 1)
            kept_ref[slot] = a
            kept_rows_ref[slot] = jnp.broadcast_to(
                jnp.concatenate([x, y], axis=1), (8, states + gauges)
            )
            s = a[:gauges, :gauges] + eye * r_row
            d_row = 1.0 / jnp.sum(eye * s, axis=0, keepdims=True)
            d_col = 1.0 / jnp.sum(eye * s, axis=1, keepdims=True)
            a_s = split(a)
            fs = (f_ref[0], f_ref[1])
            aft = dot3(a_s, (ft_ref[0], ft_ref[1]))
            nxt = dot3(fs, split(aft)) + q_ref[...]
            ct = aft[:gauges]
            if robust:
                root_row, root_col = jnp.sqrt(d_row), jnp.sqrt(d_col)
                w = gauss_jordan(s * root_col * root_row) * root_col * root_row
                wct = full(w, ct)
                pred_ref[...] = nxt - full(ct.T, wct)
                gain_ref[t + 1] = jnp.concatenate([w, wct], axis=1)
                return x, y
            e = eye - s * d_row
            es = split(e)
            u = dot3(es, es)
            c = dot3(fs, (a_s[0][:, :gauges], a_s[1][:, :gauges]))
            us = split(u)
            ed = e * d_col
            ud = u * d_col
            ct_s = split(ct)
            c_s = split(c)
            right = [ct, dot3(es, ct_s), dot3(us, ct_s)]
            left_both = dot3(c_s, split(jnp.concatenate([ed, ud], axis=1)))
            left = [c * d_row, left_both[:, :gauges], left_both[:, gauges:]]
            powers = [eye, e, u]
            if HALF_DEGREE == 4:
                ub = us[0]
                more = dot(
                    ub,
                    jnp.concatenate(
                        [right[1].astype(BF16), right[2].astype(BF16), es[0], ub], axis=1
                    ),
                )
                right += [more[:, :states], more[:, states : 2 * states]]
                powers += [
                    more[:, 2 * states : 2 * states + gauges],
                    more[:, 2 * states + gauges :],
                ]
                lb = dot(
                    jnp.concatenate(
                        [left[1].astype(BF16), left[2].astype(BF16)], axis=0
                    ),
                    ub,
                )
                left += [lb[:states], lb[states:]]
            mix = lambda cs, ms: sum(c * m for c, m in zip(cs[1:], ms[1:])) + cs[0] * ms[0]
            rt = split(mix(second, right))
            pred_ref[...] = nxt - dot3(split(mix(first, left)), rt)
            bs = split(mix(second, powers))
            poly = dot3(
                split(mix(first, powers)),
                (
                    jnp.concatenate([bs[0], rt[0]], axis=1),
                    jnp.concatenate([bs[1], rt[1]], axis=1),
                ),
            )
            poly_ref[t] = jnp.concatenate([e, poly[:, :gauges]], axis=1)
            gain_ref[t + 1] = poly * d_col
            return x, y

        zero = jnp.zeros((1, states), F32)
        x, y = lax.fori_loop(0, steps, forward, (zero, jnp.zeros((1, gauges), F32)))
        mean_step(steps, x, y)

        def backward(i, carried):
            lam, worst = carried
            t = steps - 1 - i
            slot = jnp.where(t == me, 2, 3)
            hat = jnp.broadcast_to(lam, (16, states))
            hs = split(hat)
            hat = dot3(hs, (f_ref[0], f_ref[1]))[:1]
            kept_rows_ref[slot] = jnp.broadcast_to(
                jnp.concatenate([hat, rows_ref[t + 1]], axis=1), (8, states + gauges)
            )
            gain = gain_ref[t + 1]
            kept_gain_ref[jnp.where(t == me, 0, 1)] = gain[:, :gauges]
            fix = dot3_t(hs, split(gain[:, gauges:]))[:1]
            if not robust:
                both = poly_ref[t]
                e, poly = both[:, :gauges], both[:, gauges:]
                residual = eye - poly + dot3(split(e), split(poly))
                worst = jnp.maximum(
                    worst, jnp.sum(residual * residual, axis=0, keepdims=True)
                )
            new = jnp.concatenate(
                [hat[:, :gauges] - rows_ref[t + 1] - fix, hat[:, gauges:]], axis=1
            )
            return new, worst

        nothing, worst = lax.fori_loop(
            0, steps, backward, (zero, jnp.zeros((1, gauges), F32))
        )
        return jnp.sum(worst)

    worst = run(False)

    @pl.when(jnp.logical_not(worst < RESIDUAL_LIMIT))
    def _():
        run(True)

    perm = perm_ref[...]
    a = kept_ref[0]
    w = kept_gain_ref[0]
    a_o = a[:gauges]
    r_row = step_rows(me)[1]
    s = a_o[:, :gauges] + eye * r_row
    ws = split(w)
    residual = eye - dot3(ws, split(s))
    w = w + dot(residual.astype(BF16), ws[0])
    k = dot3(split(w), split(a_o))
    cov = a - dot3(split(a[:, :gauges]), split(k))
    cov_ref[0] = move(perm_t_ref[...], move(cov, perm))
    rows, lam = kept_rows_ref[0], kept_rows_ref[2][:, :states]
    x, y = rows[:, :states], rows[:, states:]
    mean = x + dot3(split(y), split(k))
    smooth = mean - dot3(split(lam), split(cov))
    filtered_ref[...] = move(mean, perm)[:1]
    smoothed_ref[...] = move(smooth, perm)[:1]


def shards(observations, noise_var, gauge_index, dynamics, process):
    states = dynamics.shape[0]
    gauges = gauge_index.shape[0]
    steps = lax.axis_size("tm")
    vmem = pl.BlockSpec(memory_space=pltpu.VMEM)
    gathered = pl.pallas_call(
        functools.partial(gather_kernel, steps),
        out_shape=jax.ShapeDtypeStruct((steps, 1, 2 * gauges), F32),
        in_specs=[vmem] * 2,
        out_specs=vmem,
        scratch_shapes=[
            pltpu.VMEM((1, 1, 2 * gauges), F32),
            pltpu.SemaphoreType.DMA((steps,)),
            pltpu.SemaphoreType.DMA((steps,)),
        ],
        compiler_params=pltpu.CompilerParams(collective_id=0, has_side_effects=True),
    )(observations, noise_var)
    return pl.pallas_call(
        functools.partial(kernel, steps),
        out_shape=(
            jax.ShapeDtypeStruct((1, states), F32),
            jax.ShapeDtypeStruct((1, states, states), F32),
            jax.ShapeDtypeStruct((1, states), F32),
        ),
        in_specs=[vmem] * 4,
        out_specs=(vmem,) * 3,
        scratch_shapes=[
            pltpu.VMEM((2, states, states), BF16),
            pltpu.VMEM((2, states, states), BF16),
            pltpu.VMEM((states, states), F32),
            pltpu.VMEM((states, states), BF16),
            pltpu.VMEM((states, states), BF16),
            pltpu.VMEM((states, states), F32),
            pltpu.VMEM((steps + 1, gauges, gauges + states), F32),
            pltpu.VMEM((steps, gauges, 2 * gauges), F32),
            pltpu.VMEM((steps + 1, 1, gauges), F32),
            pltpu.VMEM((2, states, states), F32),
            pltpu.VMEM((2, gauges, gauges), F32),
            pltpu.VMEM((4, 8, states + gauges), F32),
            pltpu.VMEM((gauges, gauges), F32),
        ],
        compiler_params=pltpu.CompilerParams(vmem_limit_bytes=56 * 1024 * 1024),
    )(gathered, gauge_index.reshape(1, gauges), dynamics, process)


def solution(mesh):
    return jax.shard_map(
        shards,
        mesh=mesh,
        in_specs=(P(("groups", "tm"), None), P(("groups", "tm"), None), P("groups"), P(), P()),
        out_specs=(
            P(("groups", "tm"), None),
            P(("groups", "tm"), None, None),
            P(("groups", "tm"), None),
        ),
        check_vma=False,
    )
```

time: 62.6 us -> 43 us (0.69)
  blocking collectives: 23.2 us -> 0 us
  Pallas kernels: 36 us -> 42.2 us
  local copies, waits for them, and re-layouts: 2.56 us -> 0 us
    all_gather x1 -> x0, blocking collectives: 23.2 us -> none  [shards(): gathered = lax.all_gather(packed, 'tm')]
    pallas_call x0 -> x1, Pallas kernels: none -> 9.77 us  [shards(): pl.pallas_call(functools.partial(gather_kernel, steps), out_shape=jax.Sha...]
    pallas_call x1, Pallas kernels: 36 us -> 32.5 us  [shards(): pl.pallas_call(functools.partial(kernel, steps), out_shape=(jax.ShapeDtyp...]
    unnamed x10 -> x0, local copies, waits for them, and re-layouts: 2.56 us -> none
where the time goes in v2:
time: 43 us; the launch traced here: 42.9 us
  Pallas kernels  42.2 us (98%)
  between operations  0.64 us (1%)
    pallas_call x1, Pallas kernels, shards(): pl.pallas_call(functools.partial(kernel, steps), out_shape=(jax.ShapeDtyp...  32.5 us
    pallas_call x1, Pallas kernels, shards(): pl.pallas_call(functools.partial(gather_kernel, steps), out_shape=jax.Sha...  9.77 us

profile of v2, /device:TPU:0, one launch (start us, length us, event | category | flops | bytes accessed | tf_op | source)
XLA Modules:
  0.0 42.9 jit_solution(17233176691269093576)
XLA Ops:
  0.6 9.8 %shard_map.76.gathered_ref = f32[16,1,256]{2,1,0:T(1,128)} custom-call(f32[1,128]{1,0:T(1,128)} %obs_ref.1, f32[1,128]{1,0:T(1,128)} %var_ref.1), custom_call_target="tpu_custom_call" | custom-call | tf_op jit(solution)/shard_map/pallas_call | solution.py:346
  10.4 32.5 %shard_map.77 = (f32[1,256]{1,0:T(1,128)}, f32[1,256,256]{2,1,0:T(8,128)}, f32[1,256]{1,0:T(1,128)}) custom-call(f32[16,1,256]{2,1,0:T(1,128)} %shard_map.76.gathered_ref, s32[1,128]{1,0:T(1,128)} %bitcast.1, f32[256,256]{1,0:T(8,128)} %dynamics_ref.1, f32[256,256]{1,0:T(8,128)} %process_ref.1), custom_call_target="tpu_custom_call" | custom-call | tf_op jit(solution)/shard_map/pallas_call | solution.py:358

commit v3 on v2

--- a/solution.py
+++ b/solution.py
@@ -13,8 +13,8 @@
 HIGHEST = lax.Precision.HIGHEST
 MESH = pl.DeviceIdType.MESH
 RADIUS = 0.3
-HALF_DEGREE = 4
-RESIDUAL_LIMIT = 1e-6
+HALF_DEGREE = 2
+RESIDUAL_LIMIT = 4e-6
 
 
 def split(a):
@@ -91,7 +91,23 @@
     return [float(c) for c in first[::-1]], [float(c) for c in second[::-1]]
 
 
-def gather_kernel(count, obs_ref, var_ref, out_ref, row_ref, send_sem, recv_sem):
+def gather_kernel(
+    count,
+    obs_ref,
+    var_ref,
+    index_ref,
+    dynamics_ref,
+    process_ref,
+    out_ref,
+    f_ref,
+    ft_ref,
+    q_ref,
+    perm_ref,
+    perm_t_ref,
+    row_ref,
+    send_sem,
+    recv_sem,
+):
     me = lax.axis_index("tm")
     group = lax.axis_index("groups")
     gauges = obs_ref.shape[1]
@@ -106,6 +122,12 @@
     row_ref[0, :, :gauges] = obs_ref[...]
     row_ref[0, :, gauges:] = var_ref[...]
     out_ref[me] = row_ref[0]
+    states = dynamics_ref.shape[0]
+    perm_t = permutation(index_ref[...], states, gauges)
+    perm = perm_t.T.astype(BF16)
+    perm_t = perm_t.astype(BF16)
+    perm_ref[...] = perm
+    perm_t_ref[...] = perm_t
     pl.semaphore_wait(barrier, count - 1)
 
     def copy(d):
@@ -128,23 +150,24 @@
         return nothing
 
     lax.fori_loop(1, count, start, 0)
+    f = move(move(perm, dynamics_ref[...]), perm_t)
+    f_ref[0], f_ref[1] = split(f)
+    ft_ref[0], ft_ref[1] = split(f.T)
+    q_ref[...] = move(move(perm, process_ref[...]), perm_t)
     lax.fori_loop(1, count, finish, 0)
 
 
 def kernel(
     steps,
     gathered_ref,
-    index_ref,
-    dynamics_ref,
-    process_ref,
-    filtered_ref,
-    cov_ref,
-    smoothed_ref,
     f_ref,
     ft_ref,
     q_ref,
     perm_ref,
     perm_t_ref,
+    filtered_ref,
+    cov_ref,
+    smoothed_ref,
     pred_ref,
     gain_ref,
     poly_ref,
@@ -154,22 +177,12 @@
     kept_rows_ref,
     work_ref,
 ):
-    states = dynamics_ref.shape[0]
-    gauges = index_ref.shape[1]
+    states = q_ref.shape[0]
+    gauges = gathered_ref.shape[2] // 2
     me = lax.axis_index("tm")
     rg, cg = iotas((gauges, gauges))
     eye = (rg == cg).astype(F32)
     first, second = factors()
-
-    perm_t = permutation(index_ref[...], states, gauges)
-    perm = perm_t.T.astype(BF16)
-    perm_t = perm_t.astype(BF16)
-    perm_ref[...] = perm
-    perm_t_ref[...] = perm_t
-    f = move(move(perm, dynamics_ref[...]), perm_t)
-    f_ref[0], f_ref[1] = split(f)
-    ft_ref[0], ft_ref[1] = split(f.T)
-    q_ref[...] = move(move(perm, process_ref[...]), perm_t)
 
     def gauss_jordan(s):
         work_ref[...] = s
@@ -189,98 +202,79 @@
         lax.fori_loop(0, gauges, pivot, 0)
         return work_ref[...]
 
+    def mix(coefficients, terms):
+        return sum(c * m for c, m in zip(coefficients[1:], terms[1:])) + coefficients[0] * terms[0]
+
     def step_rows(t):
         row = gathered_ref[t]
         return row[:, :gauges], row[:, gauges:]
 
-    def mean_step(t, x, y):
-        g = split(gain_ref[t])
-        moved = dot3(split(jnp.broadcast_to(x, (16, states))), (ft_ref[0], ft_ref[1]))
-        gy = dot3(split(jnp.broadcast_to(y, (16, gauges))), g)
-        rows_ref[t] = gy[:1, :gauges]
-        return moved[:1] + gy[:1, gauges:]
-
     def run(robust):
         pred_ref[...] = q_ref[...]
         gain_ref[0] = jnp.zeros_like(gain_ref[0])
 
+        def gained(t, y):
+            gy = dot3_t(split(jnp.broadcast_to(y, (16, gauges))), split(gain_ref[t]))[:1]
+            rows_ref[t] = gy[:, :gauges]
+            return gy[:, gauges:]
+
         def forward(t, carried):
             x, y = carried
-            x = mean_step(t, x, y)
             obs, r_row = step_rows(t)
+            a = pred_ref[...]
+            s = a[:gauges, :gauges] + eye * r_row
+            d_row = 1.0 / jnp.sum(eye * s, axis=0, keepdims=True)
+            d_col = 1.0 / jnp.sum(eye * s, axis=1, keepdims=True)
+            fs = (f_ref[0], f_ref[1])
+            tall = jnp.concatenate([a, jnp.broadcast_to(x, (16, states))], axis=0)
+            aft = dot3(split(tall), (ft_ref[0], ft_ref[1]))
+            ct = aft[:gauges]
+            if not robust:
+                e = eye - s * d_row
+                es = split(e)
+                u = dot3(es, es)
+                us = split(u)
+                stacked = (
+                    jnp.concatenate([es[0], us[0]], axis=0),
+                    jnp.concatenate([es[1], us[1]], axis=0),
+                )
+                eu = dot3(stacked, split(ct))
+                right = [ct, eu[:gauges], eu[gauges:]]
+                powers = [eye, e, u]
+                left = (mix(first, right) * d_col).T
+                ls, rs = split(left), split(mix(second, right))
+                prod = dot3(ls, rs)
+            nxt = dot3(fs, split(aft[:states])) + q_ref[...]
+            x = aft[states : states + 1] + gained(t, y)
             y = obs - x[:, :gauges]
-            a = pred_ref[...]
             slot = jnp.where(t == me, 0, 1)
             kept_ref[slot] = a
             kept_rows_ref[slot] = jnp.broadcast_to(
                 jnp.concatenate([x, y], axis=1), (8, states + gauges)
             )
-            s = a[:gauges, :gauges] + eye * r_row
-            d_row = 1.0 / jnp.sum(eye * s, axis=0, keepdims=True)
-            d_col = 1.0 / jnp.sum(eye * s, axis=1, keepdims=True)
-            a_s = split(a)
-            fs = (f_ref[0], f_ref[1])
-            aft = dot3(a_s, (ft_ref[0], ft_ref[1]))
-            nxt = dot3(fs, split(aft)) + q_ref[...]
-            ct = aft[:gauges]
             if robust:
                 root_row, root_col = jnp.sqrt(d_row), jnp.sqrt(d_col)
                 w = gauss_jordan(s * root_col * root_row) * root_col * root_row
                 wct = full(w, ct)
                 pred_ref[...] = nxt - full(ct.T, wct)
-                gain_ref[t + 1] = jnp.concatenate([w, wct], axis=1)
+                gain_ref[t + 1] = jnp.concatenate([w, wct.T], axis=0)
                 return x, y
-            e = eye - s * d_row
-            es = split(e)
-            u = dot3(es, es)
-            c = dot3(fs, (a_s[0][:, :gauges], a_s[1][:, :gauges]))
-            us = split(u)
-            ed = e * d_col
-            ud = u * d_col
-            ct_s = split(ct)
-            c_s = split(c)
-            right = [ct, dot3(es, ct_s), dot3(us, ct_s)]
-            left_both = dot3(c_s, split(jnp.concatenate([ed, ud], axis=1)))
-            left = [c * d_row, left_both[:, :gauges], left_both[:, gauges:]]
-            powers = [eye, e, u]
-            if HALF_DEGREE == 4:
-                ub = us[0]
-                more = dot(
-                    ub,
-                    jnp.concatenate(
-                        [right[1].astype(BF16), right[2].astype(BF16), es[0], ub], axis=1
-                    ),
-                )
-                right += [more[:, :states], more[:, states : 2 * states]]
-                powers += [
-                    more[:, 2 * states : 2 * states + gauges],
-                    more[:, 2 * states + gauges :],
-                ]
-                lb = dot(
-                    jnp.concatenate(
-                        [left[1].astype(BF16), left[2].astype(BF16)], axis=0
-                    ),
-                    ub,
-                )
-                left += [lb[:states], lb[states:]]
-            mix = lambda cs, ms: sum(c * m for c, m in zip(cs[1:], ms[1:])) + cs[0] * ms[0]
-            rt = split(mix(second, right))
-            pred_ref[...] = nxt - dot3(split(mix(first, left)), rt)
-            bs = split(mix(second, powers))
-            poly = dot3(
-                split(mix(first, powers)),
+            pred_ref[...] = nxt - prod
+            ps = split(mix(first, powers) * d_col)
+            gain = dot3(
                 (
-                    jnp.concatenate([bs[0], rt[0]], axis=1),
-                    jnp.concatenate([bs[1], rt[1]], axis=1),
+                    jnp.concatenate([ps[0], ls[0]], axis=0),
+                    jnp.concatenate([ps[1], ls[1]], axis=0),
                 ),
+                split(mix(second, powers)),
             )
-            poly_ref[t] = jnp.concatenate([e, poly[:, :gauges]], axis=1)
-            gain_ref[t + 1] = poly * d_col
+            gain_ref[t + 1] = gain
+            poly_ref[t] = s
             return x, y
 
         zero = jnp.zeros((1, states), F32)
-        x, y = lax.fori_loop(0, steps, forward, (zero, jnp.zeros((1, gauges), F32)))
-        mean_step(steps, x, y)
+        x, y = lax.fori_loop(0, steps, forward, (zero, jnp.zeros((1, gauges), F32)), unroll=4)
+        gained(steps, y)
 
         def backward(i, carried):
             lam, worst = carried
@@ -293,12 +287,10 @@
                 jnp.concatenate([hat, rows_ref[t + 1]], axis=1), (8, states + gauges)
             )
             gain = gain_ref[t + 1]
-            kept_gain_ref[jnp.where(t == me, 0, 1)] = gain[:, :gauges]
-            fix = dot3_t(hs, split(gain[:, gauges:]))[:1]
+            kept_gain_ref[jnp.where(t == me, 0, 1)] = gain[:gauges]
+            fix = dot3(hs, split(gain[gauges:]))[:1]
             if not robust:
-                both = poly_ref[t]
-                e, poly = both[:, :gauges], both[:, gauges:]
-                residual = eye - poly + dot3(split(e), split(poly))
+                residual = eye - dot3(split(poly_ref[t]), split(gain[:gauges]))
                 worst = jnp.maximum(
                     worst, jnp.sum(residual * residual, axis=0, keepdims=True)
                 )
@@ -343,18 +335,27 @@
     gauges = gauge_index.shape[0]
     steps = lax.axis_size("tm")
     vmem = pl.BlockSpec(memory_space=pltpu.VMEM)
-    gathered = pl.pallas_call(
+    square = jax.ShapeDtypeStruct((states, states), BF16)
+    pair = jax.ShapeDtypeStruct((2, states, states), BF16)
+    prepared = pl.pallas_call(
         functools.partial(gather_kernel, steps),
-        out_shape=jax.ShapeDtypeStruct((steps, 1, 2 * gauges), F32),
-        in_specs=[vmem] * 2,
-        out_specs=vmem,
+        out_shape=(
+            jax.ShapeDtypeStruct((steps, 1, 2 * gauges), F32),
+            pair,
+            pair,
+            jax.ShapeDtypeStruct((states, states), F32),
+            square,
+            square,
+        ),
+        in_specs=[vmem] * 5,
+        out_specs=(vmem,) * 6,
         scratch_shapes=[
             pltpu.VMEM((1, 1, 2 * gauges), F32),
             pltpu.SemaphoreType.DMA((steps,)),
             pltpu.SemaphoreType.DMA((steps,)),
         ],
-        compiler_params=pltpu.CompilerParams(collective_id=0, has_side_effects=True),
-    )(observations, noise_var)
+        compiler_params=pltpu.CompilerParams(collective_id=0, has_side_effects=True, vmem_limit_bytes=56 * 1024 * 1024),
+    )(observations, noise_var, gauge_index.reshape(1, gauges), dynamics, process)
     return pl.pallas_call(
         functools.partial(kernel, steps),
         out_shape=(
@@ -362,17 +363,12 @@
             jax.ShapeDtypeStruct((1, states, states), F32),
             jax.ShapeDtypeStruct((1, states), F32),
         ),
-        in_specs=[vmem] * 4,
+        in_specs=[vmem] * 6,
         out_specs=(vmem,) * 3,
         scratch_shapes=[
-            pltpu.VMEM((2, states, states), BF16),
-            pltpu.VMEM((2, states, states), BF16),
             pltpu.VMEM((states, states), F32),
-            pltpu.VMEM((states, states), BF16),
-            pltpu.VMEM((states, states), BF16),
-            pltpu.VMEM((states, states), F32),
-            pltpu.VMEM((steps + 1, gauges, gauges + states), F32),
-            pltpu.VMEM((steps, gauges, 2 * gauges), F32),
+            pltpu.VMEM((steps + 1, gauges + states, gauges), F32),
+            pltpu.VMEM((steps, gauges, gauges), F32),
             pltpu.VMEM((steps + 1, 1, gauges), F32),
             pltpu.VMEM((2, states, states), F32),
             pltpu.VMEM((2, gauges, gauges), F32),
@@ -380,7 +376,7 @@
             pltpu.VMEM((gauges, gauges), F32),
         ],
         compiler_params=pltpu.CompilerParams(vmem_limit_bytes=56 * 1024 * 1024),
-    )(gathered, gauge_index.reshape(1, gauges), dynamics, process)
+    )(*prepared)
 
 
 def solution(mesh):

time: 43 us -> 35.1 us (0.82)
  Pallas kernels: 42.2 us -> 34.3 us
    pallas_call x1, Pallas kernels: 32.5 us -> 23.7 us  [shards(): pl.pallas_call(functools.partial(kernel, steps), out_shape=(jax.ShapeDtyp...]
    pallas_call x1, Pallas kernels: 9.77 us -> 10.6 us  [shards(): pl.pallas_call(functools.partial(gather_kernel, steps), out_shape=(jax.Sh...]
where the time goes in v3:
time: 35.1 us; the launch traced here: 34.9 us
  Pallas kernels  34.3 us (98%)
  between operations  0.64 us (2%)
    pallas_call x1, Pallas kernels, shards(): pl.pallas_call(functools.partial(kernel, steps), out_shape=(jax.ShapeDtyp...  23.7 us
    pallas_call x1, Pallas kernels, shards(): pl.pallas_call(functools.partial(gather_kernel, steps), out_shape=(jax.Sh...  10.6 us

profile of v3, /device:TPU:0, one launch (start us, length us, event | category | flops | bytes accessed | tf_op | source)
XLA Modules:
  0.0 34.9 jit_solution(10692447671463837497)
XLA Ops:
  0.6 10.6 %shard_map.76 = (f32[16,1,256]{2,1,0:T(1,128)}, bf16[2,256,256]{2,1,0:T(8,128)(2,1)}, bf16[2,256,256]{2,1,0:T(8,128)(2,1)}, f32[256,256]{1,0:T(8,128)}, bf16[256...) custom-call(f32[1,128]{1,0:T(1,128)} %obs_ref.1, f32[1,128]{1,0:T(1,128)} %var_ref.1, s32[1,128]{1,0:T(1,128)} %bitcast.1, ...), custom_call_target="tpu_custom_call" | custom-call | tf_op jit(solution)/shard_map/pallas_call | solution.py:340
  11.2 23.7 %shard_map.77 = (f32[1,256]{1,0:T(1,128)}, f32[1,256,256]{2,1,0:T(8,128)}, f32[1,256]{1,0:T(1,128)}) custom-call(f32[16,1,256]{2,1,0:T(1,128)} %get-tuple-element.9.gathered_ref, bf16[2,256,256]{2,1,0:T(8,128)(2,1)} %get-tuple-element.10.f_ref, bf16[2,256,256]{2,1,0:T(8,128)(2,1)} %get-tuple-element.11.ft_ref, f32[256,256]{1,0:T(8,128)} %get-tuple-element.12.q_ref, ...), custom_call_target="tpu_custom_call" | custom-call | tf_op jit(solution)/shard_map/pallas_call | solution.py:359

commit v4 on v3

--- a/solution.py
+++ b/solution.py
@@ -12,7 +12,7 @@
 BF16 = jnp.bfloat16
 HIGHEST = lax.Precision.HIGHEST
 MESH = pl.DeviceIdType.MESH
-RADIUS = 0.3
+RADIUS = 0.27
 HALF_DEGREE = 2
 RESIDUAL_LIMIT = 4e-6
 
@@ -96,8 +96,8 @@
     obs_ref,
     var_ref,
     index_ref,
-    dynamics_ref,
-    process_ref,
+    dynamics_hbm,
+    process_hbm,
     out_ref,
     f_ref,
     ft_ref,
@@ -105,6 +105,9 @@
     perm_ref,
     perm_t_ref,
     row_ref,
+    dynamics_ref,
+    process_ref,
+    load_sem,
     send_sem,
     recv_sem,
 ):
@@ -119,6 +122,12 @@
         return nothing
 
     lax.fori_loop(1, count, greet, 0)
+    loads = [
+        pltpu.make_async_copy(dynamics_hbm, dynamics_ref, load_sem.at[0]),
+        pltpu.make_async_copy(process_hbm, process_ref, load_sem.at[1]),
+    ]
+    for load in loads:
+        load.start()
     row_ref[0, :, :gauges] = obs_ref[...]
     row_ref[0, :, gauges:] = var_ref[...]
     out_ref[me] = row_ref[0]
@@ -150,6 +159,8 @@
         return nothing
 
     lax.fori_loop(1, count, start, 0)
+    for load in loads:
+        load.wait()
     f = move(move(perm, dynamics_ref[...]), perm_t)
     f_ref[0], f_ref[1] = split(f)
     ft_ref[0], ft_ref[1] = split(f.T)
@@ -300,7 +311,7 @@
             return new, worst
 
         nothing, worst = lax.fori_loop(
-            0, steps, backward, (zero, jnp.zeros((1, gauges), F32))
+            0, steps, backward, (zero, jnp.zeros((1, gauges), F32)), unroll=4
         )
         return jnp.sum(worst)
 
@@ -347,10 +358,13 @@
             square,
             square,
         ),
-        in_specs=[vmem] * 5,
+        in_specs=[vmem] * 3 + [pl.BlockSpec(memory_space=pl.ANY)] * 2,
         out_specs=(vmem,) * 6,
         scratch_shapes=[
             pltpu.VMEM((1, 1, 2 * gauges), F32),
+            pltpu.VMEM((states, states), F32),
+            pltpu.VMEM((states, states), F32),
+            pltpu.SemaphoreType.DMA((2,)),
             pltpu.SemaphoreType.DMA((steps,)),
             pltpu.SemaphoreType.DMA((steps,)),
         ],

time: 35.1 us -> 34 us (0.969)
  Pallas kernels: 34.3 us -> 33.2 us
    pallas_call x1, Pallas kernels: 23.7 us -> 23 us  [shards(): pl.pallas_call(functools.partial(kernel, steps), out_shape=(jax.ShapeDtyp...]
    pallas_call x1, Pallas kernels: 10.6 us -> 10.2 us  [shards(): pl.pallas_call(functools.partial(gather_kernel, steps), out_shape=(jax.Sh...]
where the time goes in v4:
time: 34 us; the launch traced here: 33.9 us
  Pallas kernels  33.2 us (98%)
  between operations  0.64 us (2%)
    pallas_call x1, Pallas kernels, shards(): pl.pallas_call(functools.partial(kernel, steps), out_shape=(jax.ShapeDtyp...  23 us
    pallas_call x1, Pallas kernels, shards(): pl.pallas_call(functools.partial(gather_kernel, steps), out_shape=(jax.Sh...  10.2 us

profile of v4, /device:TPU:0, one launch (start us, length us, event | category | flops | bytes accessed | tf_op | source)
XLA Modules:
  0.0 33.9 jit_solution(18223067160543096581)
XLA Ops:
  0.6 10.2 %shard_map.76 = (f32[16,1,256]{2,1,0:T(1,128)}, bf16[2,256,256]{2,1,0:T(8,128)(2,1)}, bf16[2,256,256]{2,1,0:T(8,128)(2,1)}, f32[256,256]{1,0:T(8,128)}, bf16[256...) custom-call(f32[1,128]{1,0:T(1,128)} %obs_ref.1, f32[1,128]{1,0:T(1,128)} %var_ref.1, s32[1,128]{1,0:T(1,128)} %bitcast.1, ...), custom_call_target="tpu_custom_call" | custom-call | tf_op jit(solution)/shard_map/pallas_call | solution.py:351
  10.8 23.0 %shard_map.77 = (f32[1,256]{1,0:T(1,128)}, f32[1,256,256]{2,1,0:T(8,128)}, f32[1,256]{1,0:T(1,128)}) custom-call(f32[16,1,256]{2,1,0:T(1,128)} %get-tuple-element.9.gathered_ref, bf16[2,256,256]{2,1,0:T(8,128)(2,1)} %get-tuple-element.10.f_ref, bf16[2,256,256]{2,1,0:T(8,128)(2,1)} %get-tuple-element.11.ft_ref, f32[256,256]{1,0:T(8,128)} %get-tuple-element.12.q_ref, ...), custom_call_target="tpu_custom_call" | custom-call | tf_op jit(solution)/shard_map/pallas_call | solution.py:373

commit v5 on v4

--- a/solution.py
+++ b/solution.py
@@ -254,8 +254,6 @@
                 powers = [eye, e, u]
                 left = (mix(first, right) * d_col).T
                 ls, rs = split(left), split(mix(second, right))
-                prod = dot3(ls, rs)
-            nxt = dot3(fs, split(aft[:states])) + q_ref[...]
             x = aft[states : states + 1] + gained(t, y)
             y = obs - x[:, :gauges]
             slot = jnp.where(t == me, 0, 1)
@@ -267,10 +265,18 @@
                 root_row, root_col = jnp.sqrt(d_row), jnp.sqrt(d_col)
                 w = gauss_jordan(s * root_col * root_row) * root_col * root_row
                 wct = full(w, ct)
+                nxt = dot3(fs, split(aft[:states])) + q_ref[...]
                 pred_ref[...] = nxt - full(ct.T, wct)
                 gain_ref[t + 1] = jnp.concatenate([w, wct.T], axis=0)
                 return x, y
-            pred_ref[...] = nxt - prod
+            afs = split(aft[:states])
+            pred_ref[...] = (
+                dot3(
+                    [jnp.concatenate([g, -h], axis=1) for g, h in zip(fs, ls)],
+                    [jnp.concatenate([g, h], axis=0) for g, h in zip(afs, rs)],
+                )
+                + q_ref[...]
+            )
             ps = split(mix(first, powers) * d_col)
             gain = dot3(
                 (

time: 34 us -> 33.5 us (0.985)
  Pallas kernels: 33.2 us -> 32.7 us
    pallas_call x1, Pallas kernels: 23 us -> 22.5 us  [shards(): pl.pallas_call(functools.partial(kernel, steps), out_shape=(jax.ShapeDtyp...]
where the time goes in v5:
time: 33.5 us; the launch traced here: 33.3 us
  Pallas kernels  32.7 us (98%)
  between operations  0.64 us (2%)
    pallas_call x1, Pallas kernels, shards(): pl.pallas_call(functools.partial(kernel, steps), out_shape=(jax.ShapeDtyp...  22.5 us
    pallas_call x1, Pallas kernels, shards(): pl.pallas_call(functools.partial(gather_kernel, steps), out_shape=(jax.Sh...  10.2 us

profile of v5, /device:TPU:0, one launch (start us, length us, event | category | flops | bytes accessed | tf_op | source)
XLA Modules:
  0.0 33.3 jit_solution(13590305083947902040)
XLA Ops:
  0.6 10.2 %shard_map.76 = (f32[16,1,256]{2,1,0:T(1,128)}, bf16[2,256,256]{2,1,0:T(8,128)(2,1)}, bf16[2,256,256]{2,1,0:T(8,128)(2,1)}, f32[256,256]{1,0:T(8,128)}, bf16[256...) custom-call(f32[1,128]{1,0:T(1,128)} %obs_ref.1, f32[1,128]{1,0:T(1,128)} %var_ref.1, s32[1,128]{1,0:T(1,128)} %bitcast.1, ...), custom_call_target="tpu_custom_call" | custom-call | tf_op jit(solution)/shard_map/pallas_call | solution.py:357
  10.8 22.5 %shard_map.77 = (f32[1,256]{1,0:T(1,128)}, f32[1,256,256]{2,1,0:T(8,128)}, f32[1,256]{1,0:T(1,128)}) custom-call(f32[16,1,256]{2,1,0:T(1,128)} %get-tuple-element.9.gathered_ref, bf16[2,256,256]{2,1,0:T(8,128)(2,1)} %get-tuple-element.10.f_ref, bf16[2,256,256]{2,1,0:T(8,128)(2,1)} %get-tuple-element.11.ft_ref, f32[256,256]{1,0:T(8,128)} %get-tuple-element.12.q_ref, ...), custom_call_target="tpu_custom_call" | custom-call | tf_op jit(solution)/shard_map/pallas_call | solution.py:379
